TPU v7x, 512 devices: a whole 4x4x16 slice. The times are simulated.
512 devices in a mesh: layer: 4 (over y), prow: 16 (over z), pcol: 8 (over x, core).
Axes of the slice: x: 4, y: 4, z: 16, core: 2. Of those that a mesh axis runs over, the one named last changes fastest.
Arguments:
- own_blocks: bfloat16 [4, 21, 16, 128, 2, 8, 128], P('layer', None, 'prow', None, None, 'pcol'), may hold values from -0.046875 to 0.046875
- own_pattern: int32 [4, 21, 16, 2, 8], P('layer', None, 'prow', None, 'pcol'), may hold values 0 or 1
- own_inverse: bfloat16 [4, 3, 16, 128, 2, 8, 128], P('layer', None, 'prow', None, None, 'pcol'), as said below
- pair_blocks: bfloat16 [4, 12, 16, 128, 2, 8, 128], P('layer', None, 'prow', None, None, 'pcol'), as said below
- pair_inverse: bfloat16 [4, 3, 16, 128, 2, 8, 128], P('layer', None, 'prow', None, None, 'pcol'), as said below
- root_blocks: bfloat16 [3, 16, 128, 2, 8, 128], P(None, 'prow', None, None, 'pcol'), may hold values from -0.046875 to 0.046875
- root_inverse: bfloat16 [3, 16, 128, 2, 8, 128], P(None, 'prow', None, None, 'pcol'), as said below
- own_rhs: bfloat16 [4, 3, 16, 128, 256], P('layer', None, 'prow'), may hold values from -6 to 6
- shared_rhs: bfloat16 [4, 6, 16, 128, 256], P('layer', None, 'prow'), may hold values from -3 to 3
Outputs:
- own_solution: bfloat16 [4, 3, 2, 8, 128, 256], P('layer', None, None, 'pcol')
- pair_solution: bfloat16 [4, 3, 2, 8, 128, 256], P('layer', None, None, 'pcol')
- root_solution: bfloat16 [4, 3, 2, 8, 128, 256], P('layer', None, None, 'pcol')
Inputs may be any that keep to these rules, and one draw needn't show every extreme that they name: `pair_blocks`: layers 2m and 2m+1 hold equal copies of their parent's blocks. `pair_inverse`: each panel's inverse is lower triangular; layers 2m and 2m+1 hold equal copies. `own_inverse`: each panel's inverse is lower triangular. `root_inverse`: each panel's inverse is lower triangular.
All inputs are finite; a program needn't handle non-finite values. No bound on the sum of `own_pattern` on one device may be relied on, other than what follows from the above.
Results may differ from a plain program's by a relative error of at most 0.038.
Values may be sent and summed in bfloat16 or wider, within the bound.
No kernel may reach another device: no remote copies, remote signals or barrier semaphores. Data moves between devices by JAX's collectives and lax.ppermute only.
A program may use at most 64 MiB of HBM per device.

v0:
```python
import jax
import jax.numpy as jnp
from jax import lax
from jax.sharding import PartitionSpec as P


def from_partner(array, axis, apart):
    return lax.ppermute(array, axis, [(i, i ^ 1 << apart) for i in range(lax.axis_size(axis))])


def column_product(stacked, solved):
    block_count, row_count, col_width = stacked.shape
    flattened = stacked.reshape(block_count * row_count, col_width)
    product = jnp.dot(flattened, solved, preferred_element_type=jnp.float32)
    return product.reshape(block_count, row_count, solved.shape[1])


def row_total(partial_value):
    return lax.psum(partial_value.astype(jnp.bfloat16), "pcol").astype(jnp.float32)


def panel_solve(residual, inverse):
    rounded = residual.astype(jnp.bfloat16)
    partial_value = lax.dot_general(
        inverse, rounded, (((0,), (0,)), ((), ())), preferred_element_type=jnp.float32
    )
    return lax.psum(partial_value.astype(jnp.bfloat16), "prow")


def forward_solve(
    own_cols, own_inv, pair_cols, pair_inv, root_cols, root_inv, own_rows, shared_rows
):
    panels = own_inv.shape[0]
    chain_length = 3 * panels
    first_col = lax.axis_index("pcol") == 0
    solved = []
    updates_sum = jnp.zeros((chain_length,) + own_rows.shape[1:], jnp.float32)
    offset = 0
    for step_index in range(panels):
        residual = own_rows[step_index].astype(jnp.float32)
        if step_index > 0:
            residual = residual + row_total(-updates_sum[step_index])
        panel_result = panel_solve(residual, own_inv[step_index])
        solved.append(panel_result)
        block_count = chain_length - 1 - step_index
        update = column_product(own_cols[offset : offset + block_count], panel_result)
        updates_sum = updates_sum.at[step_index + 1 :].add(update)
        offset += block_count
    ancestors = jnp.where(first_col, shared_rows.astype(jnp.float32), 0.0) - updates_sum[panels:]
    ancestors = ancestors + from_partner(ancestors.astype(jnp.bfloat16), "layer", 0).astype(
        ancestors.dtype
    )
    parent_part = ancestors[:panels]
    inner_sums = jnp.zeros_like(ancestors)
    offset = 0
    for step_index in range(panels):
        residual = row_total(parent_part[step_index] - inner_sums[step_index])
        panel_result = panel_solve(residual, pair_inv[step_index])
        solved.append(panel_result)
        block_count = 2 * panels - 1 - step_index
        update = column_product(pair_cols[offset : offset + block_count], panel_result)
        inner_sums = inner_sums.at[step_index + 1 :].add(update)
        offset += block_count
    joined = ancestors[panels:] - inner_sums[panels:]
    joined = joined + from_partner(joined.astype(jnp.bfloat16), "layer", 1).astype(joined.dtype)
    root_sums = jnp.zeros_like(joined)
    offset = 0
    for step_index in range(panels):
        residual = row_total(joined[step_index] - root_sums[step_index])
        panel_result = panel_solve(residual, root_inv[step_index])
        solved.append(panel_result)
        block_count = panels - 1 - step_index
        if block_count > 0:
            update = column_product(root_cols[offset : offset + block_count], panel_result)
            root_sums = root_sums.at[step_index + 1 :].add(update)
            offset += block_count
    return solved


def local(
    own_blocks,
    own_pattern,
    own_inverse,
    pair_blocks,
    pair_inverse,
    root_blocks,
    root_inverse,
    own_rhs,
    shared_rhs,
):
    tile_rows = own_blocks.shape[3]
    cycles = own_blocks.shape[4]
    col_width = cycles * tile_rows
    rhs_width = own_rhs.shape[-1]
    own_tiles = own_blocks.reshape(-1, tile_rows, cycles, tile_rows)
    kept_tiles = own_pattern.reshape(-1, 1, cycles, 1) > 0
    own_cols = jnp.where(kept_tiles, own_tiles, jnp.zeros((), own_tiles.dtype)).reshape(
        -1, tile_rows, col_width
    )
    pair_cols = pair_blocks.reshape(-1, tile_rows, col_width)
    root_cols = root_blocks.reshape(-1, tile_rows, col_width)
    own_inv = own_inverse.reshape(-1, tile_rows, col_width)
    pair_inv = pair_inverse.reshape(-1, tile_rows, col_width)
    root_inv = root_inverse.reshape(-1, tile_rows, col_width)
    own_rows = own_rhs.reshape(-1, tile_rows, rhs_width)
    shared_rows = shared_rhs.reshape(-1, tile_rows, rhs_width)
    panels = own_inv.shape[0]
    solved = jnp.stack(
        forward_solve(
            own_cols, own_inv, pair_cols, pair_inv, root_cols, root_inv, own_rows, shared_rows
        )
    )
    solved = solved.reshape(3 * panels, cycles, 1, tile_rows, rhs_width)
    return (solved[:panels][None], solved[panels : 2 * panels][None], solved[2 * panels :][None])


def solution(mesh):
    return jax.shard_map(
        local,
        mesh=mesh,
        in_specs=(
            P("layer", None, "prow", None, None, "pcol", None),
            P("layer", None, "prow", None, "pcol"),
            P("layer", None, "prow", None, None, "pcol", None),
            P("layer", None, "prow", None, None, "pcol", None),
            P("layer", None, "prow", None, None, "pcol", None),
            P(None, "prow", None, None, "pcol", None),
            P(None, "prow", None, None, "pcol", None),
            P("layer", None, "prow", None, None),
            P("layer", None, "prow", None, None),
        ),
        out_specs=(
            P("layer", None, None, "pcol", None, None),
            P("layer", None, None, "pcol", None, None),
            P("layer", None, None, "pcol", None, None),
        ),
        check_vma=False,
    )
```

profile of v0, /device:TPU:2, one launch (start us, length us, event | category | flops | bytes accessed | tf_op | source)
XLA Modules:
  0.0 1858.6 jit_solution(14308534549543791466)
XLA Ops:
  8.3 1.7 convolution_convert_fusion.8
  10.8 2.5 broadcast_select_fusion
  14.1 135.7 %all-reduce.18.cloned.1.call-done = bf16[256,256]{1,0:T(8,128)(2,1)} async-done(((bf16[256,256]{1,0:T(8,128)(2,1)}), bf16[256,256]{1,0:T(8,128)(2,1)}) %all-reduce.18.cloned.1.call-update) | async-done | bytes 131088 | tf_op jit(solution)/shard_map/psum | solution.py:27
  151.7 70.0 %all-reduce.20.cloned.1.call-done = bf16[128,256]{1,0:T(8,128)(2,1)} async-done(((bf16[128,256]{1,0:T(8,128)(2,1)}), bf16[128,256]{1,0:T(8,128)(2,1)}) %all-reduce.20.cloned.1.call-update) | async-done | bytes 65552 | tf_op jit(solution)/shard_map/psum | solution.py:19
  221.8 1.7 fusion.3
  225.0 135.4 %all-reduce.22.cloned.1.call-done = bf16[256,256]{0,1:T(8,128)(2,1)} async-done(((bf16[256,256]{0,1:T(8,128)(2,1)}), bf16[256,256]{0,1:T(8,128)(2,1)}) %all-reduce.22.cloned.1.call-update) | async-done | bytes 131088 | tf_op jit(solution)/shard_map/psum | solution.py:27
  362.5 69.7 %all-reduce.24.cloned.1.call-done = bf16[128,256]{1,0:T(8,128)(2,1)} async-done(((bf16[128,256]{1,0:T(8,128)(2,1)}), bf16[128,256]{1,0:T(8,128)(2,1)}) %all-reduce.24.cloned.1.call-update) | async-done | bytes 65552 | tf_op jit(solution)/shard_map/psum | solution.py:19
  432.2 1.7 fusion.4
  434.5 136.1 %all-reduce.26.cloned.1.call-done = bf16[256,256]{0,1:T(8,128)(2,1)} async-done(((bf16[256,256]{0,1:T(8,128)(2,1)}), bf16[256,256]{0,1:T(8,128)(2,1)}) %all-reduce.26.cloned.1.call-update) | async-done | bytes 131088 | tf_op jit(solution)/shard_map/psum | solution.py:27
  571.9 3.5 collective-permute-start
  575.4 6.3 collective-permute-done
  582.6 68.9 %all-reduce.28.cloned.1.call-done = bf16[128,256]{1,0:T(8,128)(2,1)} async-done(((bf16[128,256]{1,0:T(8,128)(2,1)}), bf16[128,256]{1,0:T(8,128)(2,1)}) %all-reduce.28.cloned.1.call-update) | async-done | bytes 65552 | tf_op jit(solution)/shard_map/psum | solution.py:19
  651.5 1.7 fusion.5
  653.3 136.8 %all-reduce.30.cloned.1.call-done = bf16[256,256]{0,1:T(8,128)(2,1)} async-done(((bf16[256,256]{0,1:T(8,128)(2,1)}), bf16[256,256]{0,1:T(8,128)(2,1)}) %all-reduce.30.cloned.1.call-update) | async-done | bytes 131088 | tf_op jit(solution)/shard_map/psum | solution.py:27
  792.0 70.0 %all-reduce.32.cloned.1.call-done = bf16[128,256]{1,0:T(8,128)(2,1)} async-done(((bf16[128,256]{1,0:T(8,128)(2,1)}), bf16[128,256]{1,0:T(8,128)(2,1)}) %all-reduce.32.cloned.1.call-update) | async-done | bytes 65552 | tf_op jit(solution)/shard_map/psum | solution.py:19
  862.0 1.7 fusion.6
  863.8 136.8 %all-reduce.34.cloned.1.call-done = bf16[256,256]{0,1:T(8,128)(2,1)} async-done(((bf16[256,256]{0,1:T(8,128)(2,1)}), bf16[256,256]{0,1:T(8,128)(2,1)}) %all-reduce.34.cloned.1.call-update) | async-done | bytes 131088 | tf_op jit(solution)/shard_map/psum | solution.py:27
  1002.5 69.9 %all-reduce.36.cloned.1.call-done = bf16[128,256]{1,0:T(8,128)(2,1)} async-done(((bf16[128,256]{1,0:T(8,128)(2,1)}), bf16[128,256]{1,0:T(8,128)(2,1)}) %all-reduce.36.cloned.1.call-update) | async-done | bytes 65552 | tf_op jit(solution)/shard_map/psum | solution.py:19
  1072.4 1.7 fusion.7
  1074.2 136.8 %all-reduce.38.cloned.1.call-done = bf16[256,256]{0,1:T(8,128)(2,1)} async-done(((bf16[256,256]{0,1:T(8,128)(2,1)}), bf16[256,256]{0,1:T(8,128)(2,1)}) %all-reduce.38.cloned.1.call-update) | async-done | bytes 131088 | tf_op jit(solution)/shard_map/psum | solution.py:27
  1212.3 5.0 collective-permute-start.1
  1217.3 4.1 collective-permute-done.1
  1222.5 68.8 %all-reduce.40.cloned.1.call-done = bf16[128,256]{1,0:T(8,128)(2,1)} async-done(((bf16[128,256]{1,0:T(8,128)(2,1)}), bf16[128,256]{1,0:T(8,128)(2,1)}) %all-reduce.40.cloned.1.call-update) | async-done | bytes 65552 | tf_op jit(solution)/shard_map/psum | solution.py:19
  1291.3 1.7 fusion.8
  1293.1 136.8 %all-reduce.42.cloned.1.call-done = bf16[256,256]{0,1:T(8,128)(2,1)} async-done(((bf16[256,256]{0,1:T(8,128)(2,1)}), bf16[256,256]{0,1:T(8,128)(2,1)}) %all-reduce.42.cloned.1.call-update) | async-done | bytes 131088 | tf_op jit(solution)/shard_map/psum | solution.py:27
  1431.8 69.9 %all-reduce.44.cloned.1.call-done = bf16[128,256]{1,0:T(8,128)(2,1)} async-done(((bf16[128,256]{1,0:T(8,128)(2,1)}), bf16[128,256]{1,0:T(8,128)(2,1)}) %all-reduce.44.cloned.1.call-update) | async-done | bytes 65552 | tf_op jit(solution)/shard_map/psum | solution.py:19
  1501.7 1.7 fusion.9
  1503.5 136.6 %all-reduce.46.cloned.1.call-done = bf16[256,256]{0,1:T(8,128)(2,1)} async-done(((bf16[256,256]{0,1:T(8,128)(2,1)}), bf16[256,256]{0,1:T(8,128)(2,1)}) %all-reduce.46.cloned.1.call-update) | async-done | bytes 131088 | tf_op jit(solution)/shard_map/psum | solution.py:27
  1640.2 1.8 fusion.21
  1642.2 69.7 %all-reduce.48.cloned.1.call-done = bf16[128,256]{1,0:T(8,128)(2,1)} async-done(((bf16[128,256]{1,0:T(8,128)(2,1)}), bf16[128,256]{1,0:T(8,128)(2,1)}) %all-reduce.48.cloned.1.call-update) | async-done | bytes 65552 | tf_op jit(solution)/shard_map/psum | solution.py:19
  1711.9 1.8 convolution_convert_fusion
  1715.9 134.5 %all-reduce.50.cloned.1.call-done = bf16[1,1,2,1,128,256]{5,4,3,2,1,0:T(8,128)(2,1)} async-done(((bf16[1,1,2,1,128,256]{5,4,3,2,1,0:T(8,128)(2,1)}), bf16[1,1,2,1,128,256]{5,4,3,2,1,0:T(8,128)(2,1)}) %all-reduce.50.cloned.1.call-update) | async-done | bytes 131088 | tf_op jit(solution)/shard_map/psum | solution.py:27
  (104 shorter events, 22.9 us)
Async XLA Ops:
  7.2 142.7 %all-reduce.18.cloned.1.call-start = ((), (), s32[]{:S(2)}) async-start(), calls=%async_computation | async-start | bytes 262144 | tf_op jit(solution)/shard_map/psum | solution.py:27
  10.0 211.8 %all-reduce.20.cloned.1.call-start = ((), (), s32[]{:S(2)}) async-start(), calls=%async_computation.1 | async-start | bytes 131072 | tf_op jit(solution)/shard_map/psum | solution.py:19
  151.7 208.7 %all-reduce.22.cloned.1.call-start = ((), (), s32[]{:S(2)}) async-start(), calls=%async_computation.2 | async-start | bytes 262144 | tf_op jit(solution)/shard_map/psum | solution.py:27
  223.5 208.6 %all-reduce.24.cloned.1.call-start = ((), (), s32[]{:S(2)}) async-start(), calls=%async_computation.3 | async-start | bytes 131072 | tf_op jit(solution)/shard_map/psum | solution.py:19
  361.7 208.9 %copy-start.8 = (bf16[1,6,1,128,256]{4,3,2,1,0:T(8,128)(2,1)S(1)}, bf16[1,6,1,128,256]{4,3,2,1,0:T(8,128)(2,1)}, u32[]{:S(2)}) copy-start(bf16[1,6,1,128,256]{4,3,2,1,0:T(8,128)(2,1)} %param.33) | copy-start | bytes 1179652
  362.4 208.2 %all-reduce.26.cloned.1.call-start = ((), (), s32[]{:S(2)}) async-start(), calls=%async_computation.4 | async-start | bytes 262144 | tf_op jit(solution)/shard_map/psum | solution.py:27
  433.9 217.5 %all-reduce.28.cloned.1.call-start = ((), (), s32[]{:S(2)}) async-start(), calls=%async_computation.5 | async-start | bytes 131072 | tf_op jit(solution)/shard_map/psum | solution.py:19
  571.8 10.6 copy-start.9
  571.9 9.8 collective-permute-start
  581.7 208.4 %slice-start = ((bf16[1,12,1,128,2,1,128]{6,4,5,3,2,1,0:T(2,128)(2,1)}), bf16[1,5,1,128,2,1,128]{6,4,5,3,2,1,0:T(2,128)(2,1)S(1)}, s32[]{:S(2)}) async-start(bf16[1,12,1,128,2,1,128]{6,4,5,3,2,1,0:T(2,128)(2,1)} %param.28), calls=%async_computation.17 | async-start | bytes 655360 | tf_op jit(solution)/shard_map/slice | solution.py:61
  582.4 207.7 %all-reduce.30.cloned.1.call-start = ((), (), s32[]{:S(2)}) async-start(), calls=%async_computation.6 | async-start | bytes 262144 | tf_op jit(solution)/shard_map/psum | solution.py:27
  653.2 208.8 %all-reduce.32.cloned.1.call-start = ((), (), s32[]{:S(2)}) async-start(), calls=%async_computation.7 | async-start | bytes 131072 | tf_op jit(solution)/shard_map/psum | solution.py:19
  653.2 347.4 %slice-start.1 = ((bf16[1,12,1,128,2,1,128]{6,4,5,3,2,1,0:T(2,128)(2,1)}), bf16[1,4,1,128,2,1,128]{6,4,5,3,2,1,0:T(2,128)(2,1)S(1)}, s32[]{:S(2)}) async-start(bf16[1,12,1,128,2,1,128]{6,4,5,3,2,1,0:T(2,128)(2,1)} %param.28), calls=%async_computation.18 | async-start | bytes 524288 | tf_op jit(solution)/shard_map/slice | solution.py:61
  791.9 208.7 %all-reduce.34.cloned.1.call-start = ((), (), s32[]{:S(2)}) async-start(), calls=%async_computation.8 | async-start | bytes 262144 | tf_op jit(solution)/shard_map/psum | solution.py:27
  863.7 208.7 %all-reduce.36.cloned.1.call-start = ((), (), s32[]{:S(2)}) async-start(), calls=%async_computation.9 | async-start | bytes 131072 | tf_op jit(solution)/shard_map/psum | solution.py:19
  863.8 347.2 %slice-start.2 = ((bf16[1,12,1,128,2,1,128]{6,4,5,3,2,1,0:T(2,128)(2,1)}), bf16[1,3,1,128,2,1,128]{6,4,5,3,2,1,0:T(2,128)(2,1)S(1)}, s32[]{:S(2)}) async-start(bf16[1,12,1,128,2,1,128]{6,4,5,3,2,1,0:T(2,128)(2,1)} %param.28), calls=%async_computation.19 | async-start | bytes 393216 | tf_op jit(solution)/shard_map/slice | solution.py:61
  1002.5 208.6 %all-reduce.38.cloned.1.call-start = ((), (), s32[]{:S(2)}) async-start(), calls=%async_computation.10 | async-start | bytes 262144 | tf_op jit(solution)/shard_map/psum | solution.py:27
  1074.1 217.2 %all-reduce.40.cloned.1.call-start = ((), (), s32[]{:S(2)}) async-start(), calls=%async_computation.11 | async-start | bytes 131072 | tf_op jit(solution)/shard_map/psum | solution.py:19
  1212.3 217.6 %slice-start.3 = ((bf16[3,1,128,2,1,128]{5,3,4,2,1,0:T(2,128)(2,1)}), bf16[2,1,128,2,1,128]{5,3,4,2,1,0:T(2,128)(2,1)S(1)}, s32[]{:S(2)}) async-start(bf16[3,1,128,2,1,128]{5,3,4,2,1,0:T(2,128)(2,1)} %param.30), calls=%async_computation.20 | async-start | bytes 262144 | tf_op jit(solution)/shard_map/slice | solution.py:74
  1212.3 9.2 collective-permute-start.1
  1221.6 418.6 %slice-start.4 = ((bf16[3,1,128,2,1,128]{5,3,4,2,1,0:T(2,128)(2,1)}), bf16[1,1,128,2,1,128]{5,3,4,2,1,0:T(2,128)(2,1)S(1)}, s32[]{:S(2)}) async-start(bf16[3,1,128,2,1,128]{5,3,4,2,1,0:T(2,128)(2,1)} %param.30), calls=%async_computation.21 | async-start | bytes 131072 | tf_op jit(solution)/shard_map/slice | solution.py:74
  1222.2 207.7 %all-reduce.42.cloned.1.call-start = ((), (), s32[]{:S(2)}) async-start(), calls=%async_computation.12 | async-start | bytes 262144 | tf_op jit(solution)/shard_map/psum | solution.py:27
  1222.4 419.6 %copy-start = (bf16[256,256]{0,1:T(8,128)(2,1)S(1)}, bf16[256,256]{0,1:T(8,128)(2,1)}, u32[]{:S(2)}) copy-start(bf16[256,256]{0,1:T(8,128)(2,1)} %all-reduce.22.cloned.1.call-done) | copy-start | bytes 393220
  1293.0 349.1 %copy-start.1 = (bf16[256,256]{0,1:T(8,128)(2,1)S(1)}, bf16[256,256]{0,1:T(8,128)(2,1)}, u32[]{:S(2)}) copy-start(bf16[256,256]{0,1:T(8,128)(2,1)} %all-reduce.26.cloned.1.call-done) | copy-start | bytes 393220
  1293.0 208.7 %all-reduce.44.cloned.1.call-start = ((), (), s32[]{:S(2)}) async-start(), calls=%async_computation.13 | async-start | bytes 131072 | tf_op jit(solution)/shard_map/psum | solution.py:19
  1429.9 283.8 %copy-start.7 = (bf16[256,256]{1,0:T(8,128)(2,1)S(1)}, bf16[256,256]{1,0:T(8,128)(2,1)}, u32[]{:S(2)}) copy-start(bf16[256,256]{1,0:T(8,128)(2,1)} %all-reduce.18.cloned.1.call-done) | copy-start | bytes 393220
  1431.7 208.4 %all-reduce.46.cloned.1.call-start = ((), (), s32[]{:S(2)}) async-start(), calls=%async_computation.14 | async-start | bytes 262144 | tf_op jit(solution)/shard_map/psum | solution.py:27
  1501.7 212.8 %copy-start.2 = (bf16[256,256]{0,1:T(8,128)(2,1)S(1)}, bf16[256,256]{0,1:T(8,128)(2,1)}, u32[]{:S(2)}) copy-start(bf16[256,256]{0,1:T(8,128)(2,1)} %all-reduce.30.cloned.1.call-done) | copy-start | bytes 393220
  1503.5 211.2 %copy-start.6 = (bf16[256,256]{0,1:T(8,128)(2,1)S(1)}, bf16[256,256]{0,1:T(8,128)(2,1)}, u32[]{:S(2)}) copy-start(bf16[256,256]{0,1:T(8,128)(2,1)} %all-reduce.34.cloned.1.call-done) | copy-start | bytes 393220
  1503.5 208.5 %all-reduce.48.cloned.1.call-start = ((), (), s32[]{:S(2)}) async-start(), calls=%async_computation.15 | async-start | bytes 131072 | tf_op jit(solution)/shard_map/psum | solution.py:19
  1640.2 74.6 %copy-start.3 = (bf16[256,256]{0,1:T(8,128)(2,1)S(1)}, bf16[256,256]{0,1:T(8,128)(2,1)}, u32[]{:S(2)}) copy-start(bf16[256,256]{0,1:T(8,128)(2,1)} %all-reduce.38.cloned.1.call-done) | copy-start | bytes 393220
  1642.0 208.4 %all-reduce.50.cloned.1.call-start = ((), (), s32[]{:S(2)}) async-start(), calls=%async_computation.16 | async-start | bytes 262144 | tf_op jit(solution)/shard_map/psum | solution.py:27
  (3 other events, 15.9 us)
Sparse Core Ops, SparseCore 0:
  10.9 138.9 all-reduce.17
  152.8 68.9 all-reduce.19
  224.6 135.6 all-reduce.21
  363.2 68.9 all-reduce.23
  434.9 135.6 all-reduce.25
  582.5 68.8 all-reduce.27
  654.3 135.6 all-reduce.29
  793.1 68.9 all-reduce.31
  864.9 135.6 all-reduce.33
  1003.5 68.9 all-reduce.35
  1075.3 135.6 all-reduce.37
  1222.4 68.8 all-reduce.39
  1294.2 135.6 all-reduce.41
  1432.7 68.9 all-reduce.43
  1504.4 135.6 all-reduce.45
  1643.0 68.9 all-reduce.47
  1714.7 135.6 all-reduce.49
where the time goes:
time: 1860 us
  waiting for transfers between devices  1790 us (96%)
  matrix products  25.7 us (1%)
    psum x9, waiting for transfers between devices, panel_solve(): return lax.psum(partial_value.astype(jnp.bfloat16), 'prow')  1230 us
    psum x8, waiting for transfers between devices, row_total(): lax.psum(partial_value.astype(jnp.bfloat16), 'pcol').astype(jnp.float32)  557 us
  transfers between devices with their start and end apart: 19, of which 19 were waited for; matrix products, arithmetic and copies ran while one was open for 0% of the time, Pallas kernels for 0%

commit v1 on v0

--- a/solution.py
+++ b/solution.py
@@ -2,6 +2,12 @@
 import jax.numpy as jnp
 from jax import lax
 from jax.sharding import PartitionSpec as P
+
+
+def summed_here(shard, name):
+    terms = lax.all_gather(shard, name, axis=0, tiled=False)
+    acc = terms.sum(axis=0)
+    return acc
 
 
 def from_partner(array, axis, apart):
@@ -16,7 +22,7 @@
 
 
 def row_total(partial_value):
-    return lax.psum(partial_value.astype(jnp.bfloat16), "pcol").astype(jnp.float32)
+    return summed_here(partial_value.astype(jnp.bfloat16), "pcol").astype(jnp.float32)
 
 
 def panel_solve(residual, inverse):

time: 1860 us -> 1350 us (0.73)
  waiting for transfers between devices: 1790 us -> 1190 us
  blocking collectives: 0 us -> 105 us
    psum x8 -> x0, waiting for transfers between devices: 557 us -> none  [row_total(): lax.psum(partial_value.astype(jnp.bfloat16), 'pcol').astype(jnp.float32)]
    all_gather x0 -> x8, blocking collectives: none -> 105 us  [summed_here(): terms = lax.all_gather(shard, name, axis=0, tiled=False)]
    psum x9, waiting for transfers between devices: 1230 us -> 1180 us  [panel_solve(): return lax.psum(partial_value.astype(jnp.bfloat16), 'prow')]
  transfers between devices with their start and end apart: 19 -> 11, of which waited for: 19 -> 11; matrix products, arithmetic and copies ran while one was open for 0% -> 1% of each run, Pallas kernels for 0% -> 0%
where the time goes in v1:
time: 1350 us
  waiting for transfers between devices  1190 us (88%)
  blocking collectives  105 us (8%)
  matrix products  19.9 us (1%)
  between operations  14.3 us (1%)
    psum x9, waiting for transfers between devices, panel_solve(): return lax.psum(partial_value.astype(jnp.bfloat16), 'prow')  1180 us
    all_gather x8, blocking collectives, summed_here(): terms = lax.all_gather(shard, name, axis=0, tiled=False)  105 us
  transfers between devices with their start and end apart: 11, of which 11 were waited for; matrix products, arithmetic and copies ran while one was open for 1% of the time, Pallas kernels for 0%

profile of v1, /device:TPU:2, one launch (start us, length us, event | category | flops | bytes accessed | tf_op | source)
XLA Modules:
  0.0 1351.2 jit_solution(7608456566844619697)
XLA Ops:
  8.3 1.7 convolution_convert_fusion.8
  10.8 2.5 broadcast_select_fusion
  14.1 135.7 %all-reduce.10.cloned.1.call-done = bf16[256,256]{1,0:T(8,128)(2,1)} async-done(((bf16[256,256]{1,0:T(8,128)(2,1)}), bf16[256,256]{1,0:T(8,128)(2,1)}) %all-reduce.10.cloned.1.call-update) | async-done | bytes 131088 | tf_op jit(solution)/shard_map/psum | solution.py:33
  149.8 1.2 fusion.34
  151.0 13.1 all_gather.32
  164.2 1.7 fusion.3
  167.4 129.7 %all-reduce.12.cloned.1.call-done = bf16[256,256]{0,1:T(8,128)(2,1)} async-done(((bf16[256,256]{0,1:T(8,128)(2,1)}), bf16[256,256]{0,1:T(8,128)(2,1)}) %all-reduce.12.cloned.1.call-update) | async-done | bytes 131088 | tf_op jit(solution)/shard_map/psum | solution.py:33
  297.2 1.3 convolution_add_fusion
  298.5 13.1 all_gather.33
  311.7 1.7 fusion.4
  314.1 130.6 %all-reduce.14.cloned.1.call-done = bf16[256,256]{0,1:T(8,128)(2,1)} async-done(((bf16[256,256]{0,1:T(8,128)(2,1)}), bf16[256,256]{0,1:T(8,128)(2,1)}) %all-reduce.14.cloned.1.call-update) | async-done | bytes 131088 | tf_op jit(solution)/shard_map/psum | solution.py:33
  444.7 1.2 fusion.71
  445.9 3.4 collective-permute-start
  449.4 6.1 collective-permute-done
  455.7 13.2 all_gather.34
  469.9 131.1 %all-reduce.16.cloned.1.call-done = bf16[256,256]{0,1:T(8,128)(2,1)} async-done(((bf16[256,256]{0,1:T(8,128)(2,1)}), bf16[256,256]{0,1:T(8,128)(2,1)}) %all-reduce.16.cloned.1.call-update) | async-done | bytes 131088 | tf_op jit(solution)/shard_map/psum | solution.py:33
  601.1 1.2 convolution_bitcast_fusion
  602.3 13.2 all_gather.35
  616.6 131.1 %all-reduce.18.cloned.1.call-done = bf16[256,256]{0,1:T(8,128)(2,1)} async-done(((bf16[256,256]{0,1:T(8,128)(2,1)}), bf16[256,256]{0,1:T(8,128)(2,1)}) %all-reduce.18.cloned.1.call-update) | async-done | bytes 131088 | tf_op jit(solution)/shard_map/psum | solution.py:33
  747.7 1.2 fusion.1
  748.9 13.3 all_gather.36
  763.1 131.1 %all-reduce.20.cloned.1.call-done = bf16[256,256]{0,1:T(8,128)(2,1)} async-done(((bf16[256,256]{0,1:T(8,128)(2,1)}), bf16[256,256]{0,1:T(8,128)(2,1)}) %all-reduce.20.cloned.1.call-update) | async-done | bytes 131088 | tf_op jit(solution)/shard_map/psum | solution.py:33
  895.5 4.9 collective-permute-start.1
  900.6 4.0 collective-permute-done.1
  904.7 13.1 all_gather.37
  918.8 131.1 %all-reduce.22.cloned.1.call-done = bf16[256,256]{0,1:T(8,128)(2,1)} async-done(((bf16[256,256]{0,1:T(8,128)(2,1)}), bf16[256,256]{0,1:T(8,128)(2,1)}) %all-reduce.22.cloned.1.call-update) | async-done | bytes 131088 | tf_op jit(solution)/shard_map/psum | solution.py:33
  1049.9 1.2 convolution_bitcast_fusion.3
  1051.1 13.1 all_gather.38
  1065.5 130.9 %all-reduce.24.cloned.1.call-done = bf16[256,256]{0,1:T(8,128)(2,1)} async-done(((bf16[256,256]{0,1:T(8,128)(2,1)}), bf16[256,256]{0,1:T(8,128)(2,1)}) %all-reduce.24.cloned.1.call-update) | async-done | bytes 131088 | tf_op jit(solution)/shard_map/psum | solution.py:33
  1197.5 13.3 all_gather.39
  1214.0 129.0 %all-reduce.26.cloned.1.call-done = bf16[1,1,2,1,128,256]{5,4,3,2,1,0:T(8,128)(2,1)} async-done(((bf16[1,1,2,1,128,256]{5,4,3,2,1,0:T(8,128)(2,1)}), bf16[1,1,2,1,128,256]{5,4,3,2,1,0:T(8,128)(2,1)}) %all-reduce.26.cloned.1.call-update) | async-done | bytes 131088 | tf_op jit(solution)/shard_map/psum | solution.py:33
  1343.0 1.7 pad_maximum_fusion.2
  (96 shorter events, 16.0 us)
Async XLA Ops:
  7.2 142.7 %all-reduce.10.cloned.1.call-start = ((), (), s32[]{:S(2)}) async-start(), calls=%async_computation | async-start | bytes 262144 | tf_op jit(solution)/shard_map/psum | solution.py:33
  10.0 287.2 %all-reduce.12.cloned.1.call-start = ((), (), s32[]{:S(2)}) async-start(), calls=%async_computation.1 | async-start | bytes 262144 | tf_op jit(solution)/shard_map/psum | solution.py:33
  166.0 278.7 %all-reduce.14.cloned.1.call-start = ((), (), s32[]{:S(2)}) async-start(), calls=%async_computation.2 | async-start | bytes 262144 | tf_op jit(solution)/shard_map/psum | solution.py:33
  311.6 133.0 %copy-start.8 = (bf16[1,6,1,128,256]{4,3,2,1,0:T(8,128)(2,1)S(1)}, bf16[1,6,1,128,256]{4,3,2,1,0:T(8,128)(2,1)}, u32[]{:S(2)}) copy-start(bf16[1,6,1,128,256]{4,3,2,1,0:T(8,128)(2,1)} %param.33) | copy-start | bytes 1179652
  313.5 287.6 %all-reduce.16.cloned.1.call-start = ((), (), s32[]{:S(2)}) async-start(), calls=%async_computation.3 | async-start | bytes 262144 | tf_op jit(solution)/shard_map/psum | solution.py:33
  314.1 135.2 %copy-start.9 = (bf16[1,3,1,128,2,1,128]{6,4,5,3,2,1,0:T(2,128)(2,1)S(1)}, bf16[1,3,1,128,2,1,128]{6,4,5,3,2,1,0:T(2,128)(2,1)}, u32[]{:S(2)}) copy-start(bf16[1,3,1,128,2,1,128]{6,4,5,3,2,1,0:T(2,128)(2,1)} %param.29) | copy-start | bytes 589828
  445.9 9.7 collective-permute-start
  455.6 145.4 %slice-start = ((bf16[1,12,1,128,2,1,128]{6,4,5,3,2,1,0:T(2,128)(2,1)}), bf16[1,5,1,128,2,1,128]{6,4,5,3,2,1,0:T(2,128)(2,1)S(1)}, s32[]{:S(2)}) async-start(bf16[1,12,1,128,2,1,128]{6,4,5,3,2,1,0:T(2,128)(2,1)} %param.28), calls=%async_computation.9 | async-start | bytes 655360 | tf_op jit(solution)/shard_map/slice | solution.py:67
  469.9 277.8 %all-reduce.18.cloned.1.call-start = ((), (), s32[]{:S(2)}) async-start(), calls=%async_computation.4 | async-start | bytes 262144 | tf_op jit(solution)/shard_map/psum | solution.py:33
  602.2 145.4 %slice-start.1 = ((bf16[1,12,1,128,2,1,128]{6,4,5,3,2,1,0:T(2,128)(2,1)}), bf16[1,4,1,128,2,1,128]{6,4,5,3,2,1,0:T(2,128)(2,1)S(1)}, s32[]{:S(2)}) async-start(bf16[1,12,1,128,2,1,128]{6,4,5,3,2,1,0:T(2,128)(2,1)} %param.28), calls=%async_computation.10 | async-start | bytes 524288 | tf_op jit(solution)/shard_map/slice | solution.py:67
  616.5 277.8 %all-reduce.20.cloned.1.call-start = ((), (), s32[]{:S(2)}) async-start(), calls=%async_computation.5 | async-start | bytes 262144 | tf_op jit(solution)/shard_map/psum | solution.py:33
  748.8 145.4 %slice-start.2 = ((bf16[1,12,1,128,2,1,128]{6,4,5,3,2,1,0:T(2,128)(2,1)}), bf16[1,3,1,128,2,1,128]{6,4,5,3,2,1,0:T(2,128)(2,1)S(1)}, s32[]{:S(2)}) async-start(bf16[1,12,1,128,2,1,128]{6,4,5,3,2,1,0:T(2,128)(2,1)} %param.28), calls=%async_computation.11 | async-start | bytes 393216 | tf_op jit(solution)/shard_map/slice | solution.py:67
  763.1 137.4 %copy-start.10 = (bf16[3,1,128,2,1,128]{5,3,4,2,1,0:T(2,128)(2,1)S(1)}, bf16[3,1,128,2,1,128]{5,3,4,2,1,0:T(2,128)(2,1)}, u32[]{:S(2)}) copy-start(bf16[3,1,128,2,1,128]{5,3,4,2,1,0:T(2,128)(2,1)} %param.31) | copy-start | bytes 589828
  763.1 286.8 %all-reduce.22.cloned.1.call-start = ((), (), s32[]{:S(2)}) async-start(), calls=%async_computation.6 | async-start | bytes 262144 | tf_op jit(solution)/shard_map/psum | solution.py:33
  895.5 9.1 collective-permute-start.1
  900.6 149.3 %slice-start.3 = ((bf16[3,1,128,2,1,128]{5,3,4,2,1,0:T(2,128)(2,1)}), bf16[2,1,128,2,1,128]{5,3,4,2,1,0:T(2,128)(2,1)S(1)}, s32[]{:S(2)}) async-start(bf16[3,1,128,2,1,128]{5,3,4,2,1,0:T(2,128)(2,1)} %param.30), calls=%async_computation.12 | async-start | bytes 262144 | tf_op jit(solution)/shard_map/slice | solution.py:80
  918.7 146.5 %copy-start = (bf16[256,256]{0,1:T(8,128)(2,1)S(1)}, bf16[256,256]{0,1:T(8,128)(2,1)}, u32[]{:S(2)}) copy-start(bf16[256,256]{0,1:T(8,128)(2,1)} %all-reduce.12.cloned.1.call-done) | copy-start | bytes 393220
  918.8 277.6 %all-reduce.24.cloned.1.call-start = ((), (), s32[]{:S(2)}) async-start(), calls=%async_computation.7 | async-start | bytes 262144 | tf_op jit(solution)/shard_map/psum | solution.py:33
  1049.9 15.5 %copy-start.1 = (bf16[256,256]{0,1:T(8,128)(2,1)S(1)}, bf16[256,256]{0,1:T(8,128)(2,1)}, u32[]{:S(2)}) copy-start(bf16[256,256]{0,1:T(8,128)(2,1)} %all-reduce.14.cloned.1.call-done) | copy-start | bytes 393220
  1051.1 145.3 %slice-start.4 = ((bf16[3,1,128,2,1,128]{5,3,4,2,1,0:T(2,128)(2,1)}), bf16[1,1,128,2,1,128]{5,3,4,2,1,0:T(2,128)(2,1)S(1)}, s32[]{:S(2)}) async-start(bf16[3,1,128,2,1,128]{5,3,4,2,1,0:T(2,128)(2,1)} %param.30), calls=%async_computation.13 | async-start | bytes 131072 | tf_op jit(solution)/shard_map/slice | solution.py:80
  1065.2 146.6 %copy-start.7 = (bf16[256,256]{1,0:T(8,128)(2,1)S(1)}, bf16[256,256]{1,0:T(8,128)(2,1)}, u32[]{:S(2)}) copy-start(bf16[256,256]{1,0:T(8,128)(2,1)} %all-reduce.10.cloned.1.call-done) | copy-start | bytes 393220
  1065.2 277.7 %all-reduce.26.cloned.1.call-start = ((), (), s32[]{:S(2)}) async-start(), calls=%async_computation.8 | async-start | bytes 262144 | tf_op jit(solution)/shard_map/psum | solution.py:33
  1196.4 16.2 %copy-start.2 = (bf16[256,256]{0,1:T(8,128)(2,1)S(1)}, bf16[256,256]{0,1:T(8,128)(2,1)}, u32[]{:S(2)}) copy-start(bf16[256,256]{0,1:T(8,128)(2,1)} %all-reduce.16.cloned.1.call-done) | copy-start | bytes 393220
  1197.5 15.2 %copy-start.6 = (bf16[256,256]{0,1:T(8,128)(2,1)S(1)}, bf16[256,256]{0,1:T(8,128)(2,1)}, u32[]{:S(2)}) copy-start(bf16[256,256]{0,1:T(8,128)(2,1)} %all-reduce.18.cloned.1.call-done) | copy-start | bytes 393220
  1197.5 15.3 %copy-start.3 = (bf16[256,256]{0,1:T(8,128)(2,1)S(1)}, bf16[256,256]{0,1:T(8,128)(2,1)}, u32[]{:S(2)}) copy-start(bf16[256,256]{0,1:T(8,128)(2,1)} %all-reduce.20.cloned.1.call-done) | copy-start | bytes 393220
  1210.9 2.9 copy-start.4
  1211.8 2.1 copy-start.5
Sparse Core Ops, SparseCore 0:
  10.9 138.9 all-reduce.9
  166.1 131.0 all-reduce.11
  313.6 131.0 all-reduce.13
  470.0 131.0 all-reduce.15
  616.6 130.9 all-reduce.17
  763.2 131.0 all-reduce.19
  918.9 130.9 all-reduce.21
  1065.3 131.0 all-reduce.23
  1211.9 130.9 all-reduce.25
